TPU v7x, 128 devices: a whole 4x4x4 slice. The times are simulated.
128 devices in a mesh: region: 8 (over z, core), member: 16 (over x, y).
Axes of the slice: x: 4, y: 4, z: 4, core: 2. Of those that a mesh axis runs over, the one named last changes fastest.
Arguments:
- velocity: float32 [8, 3, 131072], P(None, None, ('region', 'member')), may hold values from -6 to 6
- normals: float32 [3, 131072], P(None, ('region', 'member')), may hold values from -6 to 6
- areas: float32 [131072], P(('region', 'member')), may hold values from 0.3 to 3
- panel_nodes: int32 [131072, 4], P(('region', 'member')), may hold values from 0 to 16383, as said below
- near_blocks: bfloat16 [2048, 64, 1024], P(('region', 'member')), may hold values from -0.1875 to 0.1875
- near_cols: int32 [2048, 16], P(('region', 'member')), may hold values from 0 to 255, as said below
- near_count: int32 [2048], P(('region', 'member')), may hold values from 1 to 16
- basis_v: bfloat16 [2048, 64, 16], P(('region', 'member')), may hold values from -0.75 to 0.75
- basis_u: float32 [2048, 64, 16], P(('region', 'member')), may hold values from -1.5 to 1.5
- coupling: float32 [2048, 32, 16, 16], P(('region', 'member')), may hold values from -0.25 to 0.25
- far_cols: int32 [2048, 32], P(('region', 'member')), may hold values from 0 to 2047
Outputs:
- node_forces: float32 [8, 3, 131072], P(None, None, ('region', 'member'))
Inputs may be any that keep to these rules, and one draw needn't show every extreme that they name: `panel_nodes`: A panel's nodes lie mostly in the node range of the member that holds the panel, some in the ranges of the members beside it (the first and last members count as beside each other), a few anywhere in the region. `near_cols`: A cluster's near slots name mostly clusters of its own member, some of the members beside it (the first and last members count as beside each other), a few anywhere in the region.
All inputs are finite; a program needn't handle non-finite values.
Results may differ from a plain program's by a relative error of at most 0.0029.
Values may be sent and summed in bfloat16 or wider, within the bound.
A program may use at most 64 MiB of HBM per device.

v0:
```python
import jax
import jax.numpy as jnp
from jax import lax
from jax.sharding import PartitionSpec as P


def owned_sum(region_rows, region_nodes, node_dev):
    local_nodes = region_nodes - lax.axis_index("member") * node_dev
    inside = (local_nodes >= 0) & (local_nodes < node_dev)
    local_nodes = jnp.where(inside, local_nodes, node_dev)
    summed = jnp.zeros((node_dev, region_rows.shape[1]), jnp.float32)
    for corner in range(4):
        summed = summed.at[local_nodes[:, corner]].add(region_rows, mode="drop")
    return summed


def body(
    velocity,
    normals,
    areas,
    panel_nodes,
    near_blocks,
    near_cols,
    near_count,
    basis_v,
    basis_u,
    coupling,
    far_cols,
):
    highest = lax.Precision.HIGHEST
    loads = velocity.shape[0]
    node_dev = velocity.shape[2]
    panel_dev = normals.shape[1]
    c_dev = near_blocks.shape[0]
    block = near_blocks.shape[1]
    slots = near_cols.shape[1]
    rank = basis_v.shape[2]
    far_slots = far_cols.shape[1]
    all_motion = lax.all_gather(velocity, "member", axis=2, tiled=True)
    node_rows = all_motion.reshape(loads * 3, all_motion.shape[2]).T
    moved = jnp.zeros((panel_dev, loads * 3), jnp.float32)
    for corner in range(4):
        moved = moved + jnp.take(node_rows, panel_nodes[:, corner], axis=0)
    moved = moved.reshape(panel_dev, loads, 3)
    normal_vel = 0.25 * jnp.sum(moved * normals.T[:, None, :], axis=2)
    density = normal_vel.astype(jnp.bfloat16)
    own_blocks = jnp.transpose(density.reshape(c_dev, block, loads), (0, 2, 1))
    region_blocks = lax.all_gather(own_blocks, "member", axis=0, tiled=True)
    picked = jnp.take(region_blocks, near_cols.reshape(-1), axis=0).reshape(
        c_dev, slots, loads, block
    )
    used = jnp.arange(slots)[None, :] < near_count[:, None]
    picked = jnp.where(used[:, :, None, None], picked, jnp.zeros((), jnp.bfloat16))
    near_pot = jnp.einsum(
        "tajb,tjlb->tal",
        near_blocks.reshape(c_dev, block, slots, block),
        picked,
        preferred_element_type=jnp.float32,
    )
    coeff = jnp.einsum("tbr,tlb->trl", basis_v, own_blocks, preferred_element_type=jnp.float32)
    all_coeff = lax.all_gather(
        coeff.reshape(c_dev, rank * loads), ("region", "member"), axis=0, tiled=True
    )
    sources = jnp.take(all_coeff, far_cols.reshape(-1), axis=0).reshape(
        c_dev, far_slots, rank, loads
    )
    far_coef = jnp.einsum("tarq,taql->trl", coupling, sources, precision=highest)
    far_pot = jnp.einsum("tbr,trl->tbl", basis_u, far_coef, precision=highest)
    potential = (near_pot + far_pot).reshape(panel_dev, loads)
    weighted = (areas[None, :] * normals).T
    load_rows = (-0.25 * potential[:, :, None] * weighted[:, None, :]).reshape(panel_dev, loads * 3)
    region_rows, region_nodes = (
        lax.all_gather(load_rows, "member", axis=0, tiled=True),
        lax.all_gather(panel_nodes, "member", axis=0, tiled=True),
    )
    summed = owned_sum(region_rows, region_nodes, node_dev)
    return summed.T.reshape(loads, 3, node_dev)


def solution(mesh):
    placed = (
        P(None, None, ("region", "member")),
        P(None, ("region", "member")),
        P(("region", "member")),
        P(("region", "member"), None),
        P(("region", "member"), None, None),
        P(("region", "member"), None),
        P(("region", "member")),
        P(("region", "member"), None, None),
        P(("region", "member"), None, None),
        P(("region", "member"), None, None, None),
        P(("region", "member"), None),
    )
    return jax.shard_map(
        body,
        mesh=mesh,
        in_specs=placed,
        out_specs=P(None, None, ("region", "member")),
        check_vma=False,
    )
```

profile of v0, /device:TPU:0, one launch (start us, length us, event | category | flops | bytes accessed | tf_op | source)
XLA Modules:
  0.0 580.5 jit_solution(12812104828585175705)
XLA Ops:
  6.5 0.0 copy-start
  6.5 0.0 all-gather.4.cloned.1.call-start
  6.5 0.7 all-gather.4.cloned.1.call-update
  7.3 0.0 all-gather.6.cloned.1.call-start
  7.3 24.2 %all_gather.15 = s32[16384,4]{0,1:T(4,128)S(1)} all-gather(s32[1024,4]{0,1:T(4,128)} %param.16), channel_id=1, replica_groups=mesh['region'=8,'member'=16] {'member'}, dimensions={0}, use_global_device_ids=true | all-gather | bytes 278528 | tf_op jit(solution)/shard_map/all_gather | solution.py:74
  31.5 0.9 fusion.28
  32.5 23.4 %all-gather.4.cloned.1.call-done = f32[8,3,16384]{2,0,1:T(8,128)} async-done(((f32[8,3,1024]{2,0,1:T(8,128)}), f32[8,3,16384]{2,0,1:T(8,128)}) %all-gather.4.cloned.1.call-update) | async-done | bytes 1572880 | tf_op jit(solution)/shard_map/all_gather | solution.py:39
  55.9 3.8 copy.45
  59.7 3.6 reshape.145
  63.3 6.1 %copy.46 = f32[24,16384]{0,1:T(8,128)} copy(f32[24,16384]{1,0:T(8,128)} %reshape.145) | data formatting | bytes 3145728 | tf_op jit(solution)/shard_map/reshape | solution.py:40
  69.4 6.2 %gather_fusion.2 = f32[1024,24]{1,0:T(8,128)S(1)} fusion(f32[16384,24]{1,0:T(8,128)} %bitcast.42, s32[1024]{0:T(1024)S(1)} %fusion.22), kind=kCustom, calls=%fused_computation.clone | custom fusion | bytes 200704 | tf_op jit(solution)/shard_map/jit(_take)/gather | solution.py:43
  75.6 0.0 copy-start.3
  75.6 0.0 copy-start.2
  75.6 0.0 copy-start.5
  75.6 7.4 %gather_fusion.3 = f32[1024,24]{1,0:T(8,128)} fusion(f32[16384,24]{1,0:T(8,128)} %bitcast.43, s32[1024]{0:T(1024)S(1)} %fusion.23), kind=kCustom, calls=%fused_computation.1.clone | custom fusion | bytes 200704 | tf_op jit(solution)/shard_map/jit(_take)/gather | solution.py:43
  83.0 7.4 %gather_fusion.4 = f32[1024,24]{1,0:T(8,128)} fusion(f32[16384,24]{1,0:T(8,128)} %bitcast.44, s32[1024]{0:T(1024)S(1)} %fusion.24), kind=kCustom, calls=%fused_computation.2.clone | custom fusion | bytes 200704 | tf_op jit(solution)/shard_map/jit(_take)/gather | solution.py:43
  90.4 0.0 copy-start.4
  90.4 7.4 %gather_fusion.5 = f32[1024,24]{1,0:T(8,128)} fusion(f32[16384,24]{1,0:T(8,128)} %bitcast.45, s32[1024]{0:T(1024)S(1)} %fusion.25), kind=kCustom, calls=%fused_computation.3.clone | custom fusion | bytes 200704 | tf_op jit(solution)/shard_map/jit(_take)/gather | solution.py:43
  97.8 2.9 select_add_fusion
  100.7 0.2 copy.47
  100.9 0.0 copy-done.3
  100.9 0.1 multiply_reduce_fusion
  101.0 0.1 convert_element_type.8
  101.1 0.0 copy-done.2
  101.1 0.1 convolution_bitcast_fusion
  101.2 0.1 copy.51
  101.4 0.7 copy.52
  102.1 0.0 all-gather.6.cloned.1.call-update
  102.1 0.0 all-gather.8.cloned.1.call-start
  102.1 0.8 and_select_fusion
  102.9 0.0 copy-done.5
  102.9 0.1 reshape.147
  103.0 6.3 %reshape.148 = bf16[16,64,16,64]{3,2,1,0:T(8,128)(2,1)} reshape(bf16[16,64,1024]{2,1,0:T(8,128)(2,1)} %param.17) | data formatting | bytes 4194304 | tf_op jit(solution)/shard_map/reshape | solution.py:56
  109.4 0.0 copy-done.4
  109.4 0.1 reshape.150
  109.5 0.6 compare_and_fusion
  110.1 0.0 copy-done.7
  110.1 0.1 iota_compare_fusion
  110.2 0.0 copy-done.6
  110.2 0.0 copy-start.1
  110.2 23.5 %all_gather.17 = bf16[256,8,64]{2,1,0:T(8,128)(2,1)S(1)} all-gather(bf16[16,8,64]{2,1,0:T(8,128)(2,1)S(1)} %copy.48), channel_id=1, replica_groups=mesh['region'=8,'member'=16] {'member'}, dimensions={0}, use_global_device_ids=true | all-gather | bytes 278528 | tf_op jit(solution)/shard_map/all_gather | solution.py:48
  133.7 0.8 gather_fusion
  134.6 4.3 fusion.7
  138.8 26.4 %all-gather.6.cloned.1.call-done = f32[2048,128]{1,0:T(8,128)} async-done(((f32[16,128]{1,0:T(8,128)}), f32[2048,128]{1,0:T(8,128)}) %all-gather.6.cloned.1.call-update) | async-done | bytes 1048592 | tf_op jit(solution)/shard_map/all_gather | solution.py:61
  165.2 2.3 gather_fusion.1
  167.5 0.1 copy.53
  167.6 0.3 gather.18
  167.9 0.8 broadcast_select_fusion
  168.7 0.0 copy-done
  168.7 3.5 fusion.4
  172.2 0.0 copy-done.1
  172.2 1.1 fusion.11
  173.3 0.1 mul.69
  173.5 0.7 mul.75
  174.2 0.0 all-gather.8.cloned.1.call-update
  174.2 1.6 compare_select_fusion
  175.8 39.8 %all-gather.8.cloned.1.call-done = f32[16384,24]{0,1:T(8,128)} async-done(((f32[1024,24]{0,1:T(8,128)}), f32[16384,24]{0,1:T(8,128)}) %all-gather.8.cloned.1.call-update) | async-done | bytes 1572880 | tf_op jit(solution)/shard_map/all_gather | solution.py:73
  215.6 6.1 %copy.57 = f32[16384,24]{1,0:T(8,128)} copy(f32[16384,24]{0,1:T(8,128)} %all-gather.8.cloned.1.call-done) | data formatting | bytes 3145728 | tf_op jit(solution)/shard_map/all_gather | solution.py:73
  221.7 87.7 %scatter_custom_fusion = f32[1024,24]{1,0:T(8,128)S(1)} fusion(s32[16384]{0:T(1024)S(1)} %bitcast.53, f32[16384,24]{1,0:T(8,128)} %copy.57, f32[]{:T(128)} %constant.17.clone.1), kind=kCustom, calls=%fused_computation.35 | custom fusion | flops 393216 | bytes 98816 | tf_op jit(solution)/shard_map/scatter-add | solution.py:13
  309.5 87.8 %scatter_fusion = f32[1024,24]{1,0:T(8,128)S(1)} fusion(f32[1024,24]{1,0:T(8,128)S(1)} %scatter_custom_fusion, s32[16384]{0:T(1024)S(1)} %bitcast.50, f32[16384,24]{1,0:T(8,128)} %copy.57), kind=kCustom, calls=%fused_computation.7 | custom fusion | flops 393216 | bytes 4784128 | tf_op jit(solution)/shard_map/scatter-add | solution.py:13
  397.3 87.8 %scatter_fusion.1 = f32[1024,24]{1,0:T(8,128)S(1)} fusion(f32[1024,24]{1,0:T(8,128)S(1)} %scatter_fusion, s32[16384]{0:T(1024)S(1)} %bitcast.49, f32[16384,24]{1,0:T(8,128)} %copy.57), kind=kCustom, calls=%fused_computation.8 | custom fusion | flops 393216 | bytes 4784128 | tf_op jit(solution)/shard_map/scatter-add | solution.py:13
  485.2 87.8 %scatter_fusion.2 = f32[1024,24]{1,0:T(8,128)S(1)} fusion(f32[1024,24]{1,0:T(8,128)S(1)} %scatter_fusion.1, s32[16384]{0:T(1024)S(1)} %bitcast.48, f32[16384,24]{1,0:T(8,128)} %copy.57), kind=kCustom, calls=%fused_computation.9 | custom fusion | flops 393216 | bytes 4784128 | tf_op jit(solution)/shard_map/scatter-add | solution.py:13
  573.0 0.2 copy.61
  573.3 0.7 copy.62
  (19 shorter events, 0.2 us)
Async XLA Ops:
  6.5 162.1 %copy-start = (f32[16,32,16,16]{1,3,2,0:T(8,128)S(1)}, f32[16,32,16,16]{1,3,2,0:T(8,128)}, u32[]{:S(2)}) copy-start(f32[16,32,16,16]{1,3,2,0:T(8,128)} %param.22) | copy-start | bytes 1572868
  6.5 49.3 %all-gather.4.cloned.1.call-start = ((), (), s32[]{:S(2)}) async-start(), calls=%async_computation | async-start | bytes 1671168 | tf_op jit(solution)/shard_map/all_gather | solution.py:39
  7.3 158.0 %all-gather.6.cloned.1.call-start = ((), (), s32[]{:S(2)}) async-start(), calls=%async_computation.1 | async-start | bytes 1056768 | tf_op jit(solution)/shard_map/all_gather | solution.py:61
  75.6 25.3 %copy-start.3 = (f32[3,1024]{1,0:T(4,128)S(1)}, f32[3,1024]{1,0:T(4,128)}, u32[]{:S(2)}) copy-start(f32[3,1024]{1,0:T(4,128)} %param.14) | copy-start | bytes 36868
  75.6 25.5 %copy-start.2 = (bf16[16,64,16]{1,2,0:T(8,128)(2,1)S(1)}, bf16[16,64,16]{1,2,0:T(8,128)(2,1)}, u32[]{:S(2)}) copy-start(bf16[16,64,16]{1,2,0:T(8,128)(2,1)} %param.20) | copy-start | bytes 98308
  75.6 27.3 %copy-start.5 = (s32[16,16]{1,0:T(8,128)S(1)}, s32[16,16]{1,0:T(8,128)}, u32[]{:S(2)}) copy-start(s32[16,16]{1,0:T(8,128)} %param.18) | copy-start | bytes 3076
  90.4 19.0 %copy-start.4 = (s32[16,32]{1,0:T(8,128)S(1)}, s32[16,32]{1,0:T(8,128)}, u32[]{:S(2)}) copy-start(s32[16,32]{1,0:T(8,128)} %param.23) | copy-start | bytes 6148
  90.4 19.7 %copy-start.7 = (s32[16]{0:T(128)S(1)}, s32[16]{0:T(128)}, u32[]{:S(2)}) copy-start(s32[16]{0:T(128)} %param.19) | copy-start | bytes 196
  90.4 19.8 %copy-start.6 = (f32[1024]{0:T(1024)S(1)}, f32[1024]{0:T(1024)}, u32[]{:S(2)}) copy-start(f32[1024]{0:T(1024)} %param.15) | copy-start | bytes 12292
  102.1 113.5 %all-gather.8.cloned.1.call-start = ((), (), s32[]{:S(2)}) async-start(), calls=%async_computation.2 | async-start | bytes 1671168 | tf_op jit(solution)/shard_map/all_gather | solution.py:73
  110.2 62.0 %copy-start.1 = (f32[16,64,16]{1,2,0:T(8,128)S(1)}, f32[16,64,16]{1,2,0:T(8,128)}, u32[]{:S(2)}) copy-start(f32[16,64,16]{1,2,0:T(8,128)} %param.21) | copy-start | bytes 196612
Sparse Core Ops, SparseCore 0:
  9.6 46.2 all-gather.3
  102.2 62.9 all-gather.5
  174.3 41.2 all-gather.7
where the time goes:
time: 581 us; the launch traced here: 580 us
  other arithmetic  358 us (62%)
  waiting for transfers between devices  90.4 us (16%)
  local copies, waits for them, and re-layouts  61.7 us (11%)
  blocking collectives  47.7 us (8%)
  between operations  13.4 us (2%)
  matrix products  9.01 us (2%)
    scatter-add x4, other arithmetic, owned_sum(): summed = summed.at[local_nodes[:, corner]].add(region_rows, mode='drop')  351 us
    all_gather x1, waiting for transfers between devices, body(): lax.all_gather(load_rows, 'member', axis=0, tiled=True)  39.8 us
    gather x4, local copies, waits for them, and re-layouts, body(): moved = moved + jnp.take(node_rows, panel_nodes[:, corner], axis=0)  28.3 us
    all_gather x1, waiting for transfers between devices, body(): lax.all_gather(coeff.reshape(c_dev, rank * loads), ('region', 'member'),...  26.4 us
    all_gather x1, blocking collectives, body(): lax.all_gather(panel_nodes, 'member', axis=0, tiled=True)  24.2 us
    all_gather x1, blocking collectives, body(): region_blocks = lax.all_gather(own_blocks, 'member', axis=0, tiled=True)  23.5 us
    all_gather x1, waiting for transfers between devices, body(): all_motion = lax.all_gather(velocity, 'member', axis=2, tiled=True)  23.4 us
  transfers between devices with their start and end apart: 3, of which 3 were waited for; matrix products, arithmetic and copies ran while one was open for 3% of the time, Pallas kernels for 0%

commit v1 on v0

v1 whole, which is shorter than its diff:
```python
import functools

import jax
import jax.numpy as jnp
from jax import lax
from jax.experimental import pallas as pl
from jax.experimental.pallas import tpu as pltpu
from jax.sharding import PartitionSpec as P

MESH = pl.DeviceIdType.MESH
F32 = jnp.float32
BF16 = jnp.bfloat16
NT = (((1,), (1,)), ((), ()))


def split(x):
    high = x.astype(BF16)
    return high, (x - high.astype(F32)).astype(BF16)


def dot(a, b):
    return jnp.dot(a, b, preferred_element_type=F32)


def dot_nt(a, b):
    return lax.dot_general(a, b, NT, preferred_element_type=F32)


def kernel(
    regions,
    members,
    near_cols,
    near_count,
    far_cols,
    velocity,
    normals,
    areas,
    nodes,
    basis_v,
    basis_u,
    near_hbm,
    coupling_hbm,
    out,
    near,
    coupling,
    hot,
    motion,
    motion_cat,
    motion_low,
    moved,
    dens,
    table,
    coeffs,
    coeff_rows,
    picked_rows,
    coup_cat,
    folded,
    basis_v_wide,
    basis_u_high,
    basis_u_low,
    near_pot,
    spread_high,
    spread_low,
    force_out,
    force_in,
    load_sems,
    motion_sems,
    dens_sems,
    coeff_sems,
    column_sems,
    force_sems,
):
    region = lax.axis_index("region")
    me = lax.axis_index("member")
    clusters, block = near.shape[0], near.shape[1]
    panels = nodes.shape[1]
    loads = velocity.shape[1]

    def member_at(step):
        return lax.rem(me + step, members)

    near_load = pltpu.make_async_copy(near_hbm, near, load_sems.at[0])
    coup_load = pltpu.make_async_copy(coupling_hbm, coupling, load_sems.at[1])
    near_load.start()
    coup_load.start()

    barrier = pltpu.get_barrier_semaphore()
    for step in range(1, members):
        pl.semaphore_signal(barrier, inc=1, device_id=(region, member_at(step)), device_id_type=MESH)
    for step in range(1, regions):
        pl.semaphore_signal(
            barrier, inc=1, device_id=(lax.rem(region + step, regions), me), device_id_type=MESH
        )

    def push(source, target, sems, step):
        return pltpu.make_async_remote_copy(
            src_ref=source,
            dst_ref=target,
            send_sem=sems.at[0, step],
            recv_sem=sems.at[1, step],
            device_id=(region, member_at(step)),
            device_id_type=MESH,
        )

    own = jnp.concatenate(
        [velocity[c, :, lo * 128 : (lo + 1) * 128] for lo in range(8) for c in range(3)], axis=0
    )
    own_high, own_low = split(own)
    motion[me] = own_high
    motion_low[...] = own_low
    pl.semaphore_wait(barrier, members - 1 + regions - 1)
    motion_push = [push(motion.at[me], motion.at[me], motion_sems, s) for s in range(1, members)]
    for copy in motion_push:
        copy.start()

    node = [nodes[k : k + 1, :] for k in range(4)]
    lane_of = jnp.concatenate(
        [((n >> 10) << 7) | (n & 127) for n in node], axis=1
    )

    @pl.loop(0, hot.shape[0] // 16)
    def _(i):
        base = pl.multiple_of(i * 16, 16)
        rows = lax.broadcasted_iota(jnp.int32, (16, 4 * panels), 0) + base
        hot[pl.ds(base, 16), :] = jnp.where(rows == lane_of, 1.0, 0.0).astype(BF16)

    for g in range(clusters // 2):
        pair = jnp.concatenate([basis_v[2 * g], basis_v[2 * g + 1]], axis=1)
        basis_v_wide[:, g * 128 : (g + 1) * 128] = jnp.concatenate([pair] * loads, axis=0)
    basis_u_high[...] = jnp.zeros_like(basis_u_high)
    basis_u_low[...] = jnp.zeros_like(basis_u_low)
    empty = jnp.zeros((16, block), F32)
    for t in range(clusters):
        parts = [basis_u[t], empty] if t % 2 == 0 else [empty, basis_u[t]]
        high, low = split(jnp.concatenate(parts, axis=1))
        where = (slice(t * 16, t * 16 + 16), slice(t // 2 * 128, t // 2 * 128 + 128))
        basis_u_high[where] = high
        basis_u_low[where] = low
    coup_load.wait()

    @pl.loop(0, clusters)
    def _(t):
        high, low = split(coupling[t].reshape(256, 32))
        coup_cat[t] = jnp.concatenate([high, low], axis=1)

    table[table.shape[0] - 1] = jnp.zeros((8, 128), F32)

    for copy in motion_push:
        copy.wait_recv()
    for m in range(members):
        motion_cat[:, m * 128 : (m + 1) * 128] = motion[m]
    own_rows = pl.ds(pl.multiple_of(me * 128, 128), 128)

    @pl.loop(0, panels // 256)
    def _(i):
        base = pl.multiple_of(i * 256, 256)
        total = [jnp.zeros((8, 256), F32) for _ in range(3)]
        for k in range(4):
            columns = pl.ds(k * panels + base, 256)
            rows = dot(motion_cat[...], hot[:, columns]) + dot(motion_low[...], hot[own_rows, columns])
            lo = (nodes[k : k + 1, pl.ds(base, 256)] >> 7) & 7
            for q in range(8):
                hit = jnp.broadcast_to(lo == q, (8, 256))
                for c in range(3):
                    at = (q * 3 + c) * 8
                    total[c] = total[c] + jnp.where(hit, rows[at : at + 8], 0.0)
        for c in range(3):
            moved[c, :, pl.ds(base, 256)] = total[c]

    normal_vel = 0.25 * (
        moved[0] * normals[0:1, :] + moved[1] * normals[1:2, :] + moved[2] * normals[2:3, :]
    )
    density = normal_vel.astype(BF16).astype(F32)
    half = panels // 2
    dens[me] = jnp.concatenate([density[:, :half], density[:, half:]], axis=0).astype(BF16)
    dens_push = [push(dens.at[me], dens.at[me], dens_sems, s) for s in range(1, members)]
    lane_cluster = lax.broadcasted_iota(jnp.int32, (8, panels), 1) // block
    diagonal = jnp.concatenate(
        [jnp.where(lane_cluster == t, density, 0.0) for t in range(clusters)], axis=0
    ).astype(BF16)
    wide = dot_nt(diagonal, basis_v_wide[...])
    row_load = lax.broadcasted_iota(jnp.int32, (128, 128), 0) & 7
    lane_load = lax.broadcasted_iota(jnp.int32, (128, 128), 1) >> 4
    wide = jnp.where(row_load == lane_load, wide, 0.0)
    coeffs[me, region] = jnp.sum(wide.reshape(clusters, 8, 128), axis=1).astype(BF16)
    column_push = [
        pltpu.make_async_remote_copy(
            src_ref=coeffs.at[me, region],
            dst_ref=coeffs.at[me, region],
            send_sem=column_sems.at[0, s],
            recv_sem=column_sems.at[1, s],
            device_id=(lax.rem(region + s, regions), me),
            device_id_type=MESH,
        )
        for s in range(1, regions)
    ]
    for copy in column_push:
        copy.start()
    for copy in dens_push:
        copy.start()
    for copy in column_push:
        copy.wait_recv()
    coeff_push = [push(coeffs.at[me], coeffs.at[me], coeff_sems, s) for s in range(1, members)]
    for copy in coeff_push:
        copy.start()

    near_load.wait()
    for copy in dens_push:
        copy.wait_recv()
    left = lax.broadcasted_iota(jnp.int32, (8, 128), 1) < block

    @pl.loop(0, members)
    def _(m):
        rows = dens[m].astype(F32)
        for h in range(2):
            for g in range(half // 128):
                both = rows[h * 8 : h * 8 + 8, g * 128 : (g + 1) * 128]
                turned = pltpu.roll(both, block, axis=1)
                at = m * clusters + h * (clusters // 2) + g * 2
                table[at] = jnp.where(left, both, turned)
                table[at + 1] = jnp.where(left, turned, both)

    slots = near_cols.shape[1]
    unused = table.shape[0] - 1

    @pl.loop(0, clusters // 2)
    def _(g):
        picked = []
        for h in range(2):
            t = 2 * g + h
            count = near_count[t]
            parts = []
            for j in range(0, slots, 2):
                first = jnp.where(j < count, near_cols[t, j], unused)
                second = jnp.where(j + 1 < count, near_cols[t, j + 1], unused)
                parts.append(jnp.where(left, table[first], table[second]))
            picked.append(jnp.concatenate(parts, axis=1))
        both = jnp.concatenate(picked, axis=0).astype(BF16)
        blocks = near[pl.ds(2 * g, 2)].reshape(2 * block, slots * block)
        result = dot_nt(both, blocks)
        near_pot[:, pl.ds(pl.multiple_of(g * 128, 128), 128)] = jnp.where(left, result[:8], result[8:])

    for copy in coeff_push:
        copy.wait_recv()

    @pl.loop(0, members)
    def _(m):
        for r in range(regions):
            at = pl.multiple_of((r * members + m) * clusters, clusters)
            coeff_rows[pl.ds(at, clusters), :] = coeffs[m, r].astype(F32)

    own_q = lax.broadcasted_iota(jnp.int32, (256, 128), 0) & 15
    lane_q = lax.broadcasted_iota(jnp.int32, (256, 128), 1) & 15
    same_q = own_q == lane_q

    @pl.loop(0, clusters)
    def _(t):
        for a in range(32):
            picked_rows[pl.ds(a, 1), :] = coeff_rows[pl.ds(far_cols[t, a], 1), :]
        rows = picked_rows[...].astype(BF16)
        product = dot(coup_cat[t], jnp.concatenate([rows, rows], axis=0))
        product = jnp.where(same_q, product, 0.0)
        folded[pl.ds(pl.multiple_of(t * 16, 16), 16), :] = jnp.sum(
            product.reshape(16, 16, 128), axis=1
        )

    fold = jnp.where(
        lax.broadcasted_iota(jnp.int32, (8, 128), 0)
        == lax.broadcasted_iota(jnp.int32, (8, 128), 1) >> 4,
        1.0,
        0.0,
    )
    fold = jnp.concatenate([fold, fold], axis=0).astype(BF16)
    folded_high, folded_low = split(folded[...])
    far_coef = (dot_nt(fold, folded_high) + dot_nt(fold, folded_low))[:8]
    far_high, far_low = split(far_coef)
    far_both = jnp.concatenate([far_high.astype(F32), far_low.astype(F32)], axis=0).astype(BF16)
    with_high = dot(far_both, basis_u_high[...])
    with_low = dot(far_both, basis_u_low[...])
    potential = near_pot[...] + (with_high[:8] + with_high[8:] + with_low[:8])

    scaled = -0.25 * areas[...]
    for c in range(3):
        moved[c] = potential * (scaled * normals[c : c + 1, :])

    @pl.loop(0, panels // 256)
    def _(i):
        base = pl.multiple_of(i * 256, 256)
        load = [moved[c, :, pl.ds(base, 256)] for c in range(3)]
        for k in range(4):
            lo = (nodes[k : k + 1, pl.ds(base, 256)] >> 7) & 7
            rows = []
            for q in range(8):
                hit = jnp.broadcast_to(lo == q, (8, 256))
                rows += [jnp.where(hit, load[c], 0.0) for c in range(3)]
            high, low = split(jnp.concatenate(rows, axis=0))
            columns = pl.ds(k * panels + base, 256)
            spread_high[:, columns] = high
            spread_low[:, columns] = low

    pairs = members // 2
    pair = me // 2

    @pl.loop(1, pairs)
    def _(i):
        other = lax.rem(pair + i, pairs)
        rows = hot[pl.ds(pl.multiple_of(other * 256, 256), 256), :]
        sums = dot_nt(spread_high[...], rows).astype(BF16)
        for h in range(2):
            target = 2 * other + h
            step = lax.rem(target - me + members, members)
            force_out[target] = sums[:, h * 128 : (h + 1) * 128]
            push_force(force_out, force_in, force_sems, region, me, target, step).start()

    partner = me + 1 - 2 * lax.rem(me, 2)
    partner_rows = pl.ds(pl.multiple_of(partner * 128, 128), 128)
    force_out[partner] = dot_nt(spread_high[...], hot[partner_rows, :]).astype(BF16)
    step = lax.rem(partner - me + members, members)
    push_force(force_out, force_in, force_sems, region, me, partner, step).start()
    mine = hot[own_rows, :]
    total = dot_nt(spread_high[...], mine) + dot_nt(spread_low[...], mine)
    for step in range(1, members):
        source = lax.rem(me - step + members, members)
        push_force(force_out, force_in, force_sems, region, me, member_at(step), step).wait_recv()
        total = total + force_in[source].astype(F32)
    for lo in range(8):
        for c in range(3):
            at = (lo * 3 + c) * 8
            out[c, :, lo * 128 : (lo + 1) * 128] = total[at : at + 8]

    for copy in motion_push + dens_push + column_push + coeff_push:
        copy.wait_send()
    for step in range(1, members):
        push_force(force_out, force_in, force_sems, region, me, member_at(step), step).wait_send()


def push_force(force_out, force_in, sems, region, me, target, step):
    return pltpu.make_async_remote_copy(
        src_ref=force_out.at[target],
        dst_ref=force_in.at[me],
        send_sem=sems.at[0, step],
        recv_sem=sems.at[1, step],
        device_id=(region, target),
        device_id_type=MESH,
    )


def body(
    regions,
    members,
    velocity,
    normals,
    areas,
    panel_nodes,
    near_blocks,
    near_cols,
    near_count,
    basis_v,
    basis_u,
    coupling,
    far_cols,
):
    nodes = velocity.shape[2]
    panels = normals.shape[1]
    clusters, block = near_blocks.shape[0], near_blocks.shape[1]
    rows = 24 * nodes // 128
    lanes = members * 128
    smem = pl.BlockSpec(memory_space=pltpu.SMEM)
    vmem = pl.BlockSpec(memory_space=pltpu.VMEM)
    hbm = pl.BlockSpec(memory_space=pl.ANY)
    dma = pltpu.SemaphoreType.DMA
    result = pl.pallas_call(
        functools.partial(kernel, regions, members),
        out_shape=jax.ShapeDtypeStruct((3, 8, nodes), F32),
        in_specs=[smem] * 3 + [vmem] * 6 + [hbm] * 2,
        out_specs=vmem,
        scratch_shapes=[
            pltpu.VMEM(near_blocks.shape, BF16),
            pltpu.VMEM((clusters, 16, 16, 32), F32),
            pltpu.VMEM((lanes, 4 * panels), BF16),
            pltpu.VMEM((members, rows, 128), BF16),
            pltpu.VMEM((rows, lanes), BF16),
            pltpu.VMEM((rows, 128), BF16),
            pltpu.VMEM((3, 8, panels), F32),
            pltpu.VMEM((members, 16, panels // 2), BF16),
            pltpu.VMEM((members * clusters + 1, 8, 128), F32),
            pltpu.VMEM((members, regions, clusters, 128), BF16),
            pltpu.VMEM((members * regions * clusters, 128), F32),
            pltpu.VMEM((32, 128), F32),
            pltpu.VMEM((clusters, 256, 64), BF16),
            pltpu.VMEM((clusters * 16, 128), F32),
            pltpu.VMEM((128, panels), BF16),
            pltpu.VMEM((clusters * 16, panels), BF16),
            pltpu.VMEM((clusters * 16, panels), BF16),
            pltpu.VMEM((8, panels), F32),
            pltpu.VMEM((rows, 4 * panels), BF16),
            pltpu.VMEM((rows, 4 * panels), BF16),
            pltpu.VMEM((members, rows, 128), BF16),
            pltpu.VMEM((members, rows, 128), BF16),
            dma((2,)),
            dma((2, members)),
            dma((2, members)),
            dma((2, members)),
            dma((2, regions)),
            dma((2, members)),
        ],
        compiler_params=pltpu.CompilerParams(
            collective_id=0, has_side_effects=True, vmem_limit_bytes=56 * 1024 * 1024
        ),
        name="hull",
    )(
        near_cols,
        near_count,
        far_cols,
        jnp.transpose(velocity, (1, 0, 2)),
        normals,
        areas.reshape(1, panels),
        panel_nodes.T,
        jnp.transpose(basis_v, (0, 2, 1)),
        jnp.transpose(basis_u, (0, 2, 1)),
        near_blocks,
        jnp.transpose(coupling, (0, 2, 3, 1)),
    )
    return jnp.transpose(result, (1, 0, 2))


def solution(mesh):
    both = ("region", "member")
    placed = (
        P(None, None, both),
        P(None, both),
        P(both),
        P(both, None),
        P(both, None, None),
        P(both, None),
        P(both),
        P(both, None, None),
        P(both, None, None),
        P(both, None, None, None),
        P(both, None),
    )
    return jax.shard_map(
        functools.partial(body, mesh.shape["region"], mesh.shape["member"]),
        mesh=mesh,
        in_specs=placed,
        out_specs=P(None, None, both),
        check_vma=False,
    )
```

time: 581 us -> 61.3 us (0.11)
  other arithmetic: 358 us -> 0 us
  waiting for transfers between devices: 90.4 us -> 0 us
  local copies, waits for them, and re-layouts: 61.7 us -> 1.54 us
  Pallas kernels: 0 us -> 58.9 us
  blocking collectives: 47.7 us -> 0 us
  between operations: 13.4 us -> 0.01 us
  matrix products: 9.01 us -> 0 us
    scatter-add x4 -> x0, other arithmetic: 351 us -> none  [owned_sum(): summed = summed.at[local_nodes[:, corner]].add(region_rows, mode='drop')]
    all_gather x3 -> x0, waiting for transfers between devices: 89.6 us -> none  [the longest x1 39.8 us: body(): lax.all_gather(load_rows, 'member', axis=0, tiled=True)]
    pallas_call x0 -> x1, Pallas kernels: none -> 58.9 us  [body(): pl.pallas_call(functools.partial(kernel, regions, members), out_shape=jax...]
    all_gather x2 -> x0, blocking collectives: 47.7 us -> none  [the longest x1 24.2 us: body(): lax.all_gather(panel_nodes, 'member', axis=0, tiled=True)]
    gather x8 -> x0, local copies, waits for them, and re-layouts: 31.8 us -> none  [the longest x4 28.3 us: body(): moved = moved + jnp.take(node_rows, panel_nodes[:, corner], axis=0)]
    reshape x9 -> x0, local copies, waits for them, and re-layouts: 17.7 us -> none  [the longest x2 9.7 us: body(): node_rows = all_motion.reshape(loads * 3, all_motion.shape[2]).T]
    all_gather x2 -> x0, local copies, waits for them, and re-layouts: 9.94 us -> none  [the longest x1 6.11 us: body(): lax.all_gather(load_rows, 'member', axis=0, tiled=True)]
    dot_general x4 -> x0, matrix products: 9.01 us -> none  [the longest x1 4.25 us: body(): jnp.einsum('tajb,tjlb->tal', near_blocks.reshape(c_dev, block, slots, blo...]
  transfers between devices with their start and end apart: 3 -> 0, of which waited for: 3 -> 0; matrix products, arithmetic and copies ran while one was open for 3% -> 0% of each run, Pallas kernels for 0% -> 0%
where the time goes in v1:
time: 61.3 us; the launch traced here: 60.4 us
  Pallas kernels  58.9 us (96%)
  local copies, waits for them, and re-layouts  1.54 us (3%)
    pallas_call x1, Pallas kernels, body(): pl.pallas_call(functools.partial(kernel, regions, members), out_shape=jax...  58.9 us
    unnamed x1, local copies, waits for them, and re-layouts  1.54 us

profile of v1, /device:TPU:0, one launch (start us, length us, event | category | flops | bytes accessed | tf_op | source)
XLA Modules:
  0.0 60.4 jit_solution(8143486828209823444)
XLA Ops:
  0.0 58.9 %hull.1 = f32[3,8,1024]{2,1,0:T(8,128)} custom-call(s32[16,16]{1,0:T(8,128)} %near_cols.1, s32[16]{0:T(128)} %near_count.1, s32[16,32]{1,0:T(8,128)} %far_cols.1, f32[3,8,1024]{2,1,0:T(8,128)} %bitcast.10, f32[3,1024]{1,0:T(4,128)} %normals.1, f32[1,1024]{1,0:T(1,128)} %bitcast.13, s32[4,1024]{1,0:T(4,128)} %bitcast.12, bf16[16,16,64]{2,1,0:T(8,128)(2,1)} %bitcast.11, ...), custom_call_target="tpu_custom_call" | custom-call | tf_op jit(solution)/shard_map/hull/pallas_call | solution.py:372
  58.9 1.5 %copy.13 = f32[8,3,1024]{2,0,1:T(8,128)} copy(f32[8,3,1024]{2,0,1:T(8,128)} %bitcast.8) | data formatting | bytes 196608

commit v2 on v1

--- a/solution.py
+++ b/solution.py
@@ -44,6 +44,8 @@
     near,
     coupling,
     hot,
+    hot_turned,
+    column_of,
     motion,
     motion_cat,
     motion_low,
@@ -61,14 +63,15 @@
     near_pot,
     spread_high,
     spread_low,
+    force_near,
     force_out,
     force_in,
     load_sems,
     motion_sems,
     dens_sems,
     coeff_sems,
-    column_sems,
     force_sems,
+    ready,
 ):
     region = lax.axis_index("region")
     me = lax.axis_index("member")
@@ -93,14 +96,16 @@
         )
 
     def push(source, target, sems, step):
-        return pltpu.make_async_remote_copy(
-            src_ref=source,
-            dst_ref=target,
-            send_sem=sems.at[0, step],
-            recv_sem=sems.at[1, step],
-            device_id=(region, member_at(step)),
-            device_id_type=MESH,
-        )
+        return push_to(source, target, sems, region, member_at(step))
+
+    def push_all(rows, sems):
+        @pl.loop(1, members)
+        def _(step):
+            push(rows.at[me], rows.at[me], sems, step).start()
+
+    def pushed(rows, sems):
+        part = rows.at[pl.ds(0, members - 1)]
+        return push(part, part, sems, 1)
 
     own = jnp.concatenate(
         [velocity[c, :, lo * 128 : (lo + 1) * 128] for lo in range(8) for c in range(3)], axis=0
@@ -109,20 +114,42 @@
     motion[me] = own_high
     motion_low[...] = own_low
     pl.semaphore_wait(barrier, members - 1 + regions - 1)
-    motion_push = [push(motion.at[me], motion.at[me], motion_sems, s) for s in range(1, members)]
-    for copy in motion_push:
-        copy.start()
-
-    node = [nodes[k : k + 1, :] for k in range(4)]
-    lane_of = jnp.concatenate(
-        [((n >> 10) << 7) | (n & 127) for n in node], axis=1
-    )
-
-    @pl.loop(0, hot.shape[0] // 16)
+    push_all(motion, motion_sems)
+    for step in range(1, regions):
+        pl.semaphore_signal(
+            ready, inc=1, device_id=(lax.rem(region + step, regions), me), device_id_type=MESH
+        )
+
+    node = nodes[...]
+    lanes_low, owner = (node & 127).astype(F32), (node >> 10).astype(F32)
+    column_of[...] = jnp.transpose(jnp.concatenate([lanes_low, owner], axis=0))
+    one, zero = jnp.ones((), BF16), jnp.zeros((), BF16)
+
+    @pl.loop(0, 8)
     def _(i):
         base = pl.multiple_of(i * 16, 16)
-        rows = lax.broadcasted_iota(jnp.int32, (16, 4 * panels), 0) + base
-        hot[pl.ds(base, 16), :] = jnp.where(rows == lane_of, 1.0, 0.0).astype(BF16)
+        rows = (lax.broadcasted_iota(jnp.int32, (16, panels), 0) + base).astype(F32).astype(BF16)
+        for k in range(4):
+            low = jnp.broadcast_to(lanes_low[k : k + 1], (16, panels)).astype(BF16)
+            holder = jnp.broadcast_to(owner[k : k + 1], (16, panels)).astype(BF16)
+            found = jnp.where(low == rows, one, zero)
+            for m in range(members):
+                hot[pl.ds(m * 128 + base, 16), k * panels : (k + 1) * panels] = jnp.where(
+                    holder == float(m), found, zero
+                )
+
+    @pl.loop(0, panels // 16)
+    def _(i):
+        base = pl.multiple_of(i * 16, 16)
+        lanes = lax.broadcasted_iota(jnp.int32, (16, 128), 1).astype(F32).astype(BF16)
+        for k in range(4):
+            low = jnp.broadcast_to(column_of[pl.ds(base, 16), k : k + 1], (16, 128)).astype(BF16)
+            holder = jnp.broadcast_to(column_of[pl.ds(base, 16), k + 4 : k + 5], (16, 128)).astype(BF16)
+            found = jnp.where(low == lanes, one, zero)
+            for m in range(members):
+                hot_turned[pl.ds(k * panels + base, 16), m * 128 : (m + 1) * 128] = jnp.where(
+                    holder == float(m), found, zero
+                )
 
     for g in range(clusters // 2):
         pair = jnp.concatenate([basis_v[2 * g], basis_v[2 * g + 1]], axis=1)
@@ -145,27 +172,25 @@
 
     table[table.shape[0] - 1] = jnp.zeros((8, 128), F32)
 
-    for copy in motion_push:
-        copy.wait_recv()
+    pushed(motion, motion_sems).wait_recv()
     for m in range(members):
         motion_cat[:, m * 128 : (m + 1) * 128] = motion[m]
     own_rows = pl.ds(pl.multiple_of(me * 128, 128), 128)
 
-    @pl.loop(0, panels // 256)
-    def _(i):
-        base = pl.multiple_of(i * 256, 256)
-        total = [jnp.zeros((8, 256), F32) for _ in range(3)]
-        for k in range(4):
-            columns = pl.ds(k * panels + base, 256)
-            rows = dot(motion_cat[...], hot[:, columns]) + dot(motion_low[...], hot[own_rows, columns])
-            lo = (nodes[k : k + 1, pl.ds(base, 256)] >> 7) & 7
+    for c in range(3):
+        moved[c] = jnp.zeros((8, panels), F32)
+
+    @pl.loop(0, 4)
+    def _(k):
+        columns = pl.ds(pl.multiple_of(k * panels, panels), panels)
+        rows = dot(motion_cat[...], hot[:, columns]) + dot(motion_low[...], hot[own_rows, columns])
+        lo = (nodes[pl.ds(k, 1), :] >> 7) & 7
+        for c in range(3):
+            total = moved[c]
             for q in range(8):
-                hit = jnp.broadcast_to(lo == q, (8, 256))
-                for c in range(3):
-                    at = (q * 3 + c) * 8
-                    total[c] = total[c] + jnp.where(hit, rows[at : at + 8], 0.0)
-        for c in range(3):
-            moved[c, :, pl.ds(base, 256)] = total[c]
+                at = (q * 3 + c) * 8
+                total = total + jnp.where(jnp.broadcast_to(lo == q, (8, panels)), rows[at : at + 8], 0.0)
+            moved[c] = total
 
     normal_vel = 0.25 * (
         moved[0] * normals[0:1, :] + moved[1] * normals[1:2, :] + moved[2] * normals[2:3, :]
@@ -173,7 +198,8 @@
     density = normal_vel.astype(BF16).astype(F32)
     half = panels // 2
     dens[me] = jnp.concatenate([density[:, :half], density[:, half:]], axis=0).astype(BF16)
-    dens_push = [push(dens.at[me], dens.at[me], dens_sems, s) for s in range(1, members)]
+    push_all(dens, dens_sems)
+
     lane_cluster = lax.broadcasted_iota(jnp.int32, (8, panels), 1) // block
     diagonal = jnp.concatenate(
         [jnp.where(lane_cluster == t, density, 0.0) for t in range(clusters)], axis=0
@@ -182,31 +208,17 @@
     row_load = lax.broadcasted_iota(jnp.int32, (128, 128), 0) & 7
     lane_load = lax.broadcasted_iota(jnp.int32, (128, 128), 1) >> 4
     wide = jnp.where(row_load == lane_load, wide, 0.0)
-    coeffs[me, region] = jnp.sum(wide.reshape(clusters, 8, 128), axis=1).astype(BF16)
-    column_push = [
-        pltpu.make_async_remote_copy(
-            src_ref=coeffs.at[me, region],
-            dst_ref=coeffs.at[me, region],
-            send_sem=column_sems.at[0, s],
-            recv_sem=column_sems.at[1, s],
-            device_id=(lax.rem(region + s, regions), me),
-            device_id_type=MESH,
-        )
-        for s in range(1, regions)
-    ]
-    for copy in column_push:
-        copy.start()
-    for copy in dens_push:
-        copy.start()
-    for copy in column_push:
-        copy.wait_recv()
-    coeff_push = [push(coeffs.at[me], coeffs.at[me], coeff_sems, s) for s in range(1, members)]
-    for copy in coeff_push:
-        copy.start()
+    device = region * members + me
+    coeffs[device] = jnp.sum(wide.reshape(clusters, 8, 128), axis=1).astype(BF16)
+    pl.semaphore_wait(ready, regions - 1)
+
+    @pl.loop(1, regions * members)
+    def _(step):
+        there = lax.rem(region + step // members, regions)
+        push_to(coeffs.at[device], coeffs.at[device], coeff_sems, there, member_at(lax.rem(step, members))).start()
 
     near_load.wait()
-    for copy in dens_push:
-        copy.wait_recv()
+    pushed(dens, dens_sems).wait_recv()
     left = lax.broadcasted_iota(jnp.int32, (8, 128), 1) < block
 
     @pl.loop(0, members)
@@ -240,14 +252,16 @@
         result = dot_nt(both, blocks)
         near_pot[:, pl.ds(pl.multiple_of(g * 128, 128), 128)] = jnp.where(left, result[:8], result[8:])
 
-    for copy in coeff_push:
-        copy.wait_recv()
+    coeff_part = coeffs.at[pl.ds(0, regions * members - 1)]
+    coeff_pushed = push(coeff_part, coeff_part, coeff_sems, 1)
+    coeff_pushed.wait_recv()
 
     @pl.loop(0, members)
-    def _(m):
+    def _(i):
         for r in range(regions):
-            at = pl.multiple_of((r * members + m) * clusters, clusters)
-            coeff_rows[pl.ds(at, clusters), :] = coeffs[m, r].astype(F32)
+            d = i * regions + r
+            at = pl.multiple_of(d * clusters, clusters)
+            coeff_rows[pl.ds(at, clusters), :] = coeffs[d].astype(F32)
 
     own_q = lax.broadcasted_iota(jnp.int32, (256, 128), 0) & 15
     lane_q = lax.broadcasted_iota(jnp.int32, (256, 128), 1) & 15
@@ -256,13 +270,13 @@
     @pl.loop(0, clusters)
     def _(t):
         for a in range(32):
-            picked_rows[pl.ds(a, 1), :] = coeff_rows[pl.ds(far_cols[t, a], 1), :]
-        rows = picked_rows[...].astype(BF16)
+            picked_rows[pl.ds(t * 32 + a, 1), :] = coeff_rows[pl.ds(far_cols[t, a], 1), :]
+
+    for t in range(clusters):
+        rows = picked_rows[t * 32 : t * 32 + 32].astype(BF16)
         product = dot(coup_cat[t], jnp.concatenate([rows, rows], axis=0))
         product = jnp.where(same_q, product, 0.0)
-        folded[pl.ds(pl.multiple_of(t * 16, 16), 16), :] = jnp.sum(
-            product.reshape(16, 16, 128), axis=1
-        )
+        folded[t * 16 : t * 16 + 16] = jnp.sum(product.reshape(16, 16, 128), axis=1)
 
     fold = jnp.where(
         lax.broadcasted_iota(jnp.int32, (8, 128), 0)
@@ -298,49 +312,47 @@
             spread_high[:, columns] = high
             spread_low[:, columns] = low
 
-    pairs = members // 2
-    pair = me // 2
-
-    @pl.loop(1, pairs)
+    groups = members // 4
+    group = me // 4
+
+    @pl.loop(1, groups + 1)
     def _(i):
-        other = lax.rem(pair + i, pairs)
-        rows = hot[pl.ds(pl.multiple_of(other * 256, 256), 256), :]
-        sums = dot_nt(spread_high[...], rows).astype(BF16)
-        for h in range(2):
-            target = 2 * other + h
-            step = lax.rem(target - me + members, members)
-            force_out[target] = sums[:, h * 128 : (h + 1) * 128]
-            push_force(force_out, force_in, force_sems, region, me, target, step).start()
-
-    partner = me + 1 - 2 * lax.rem(me, 2)
-    partner_rows = pl.ds(pl.multiple_of(partner * 128, 128), 128)
-    force_out[partner] = dot_nt(spread_high[...], hot[partner_rows, :]).astype(BF16)
-    step = lax.rem(partner - me + members, members)
-    push_force(force_out, force_in, force_sems, region, me, partner, step).start()
-    mine = hot[own_rows, :]
-    total = dot_nt(spread_high[...], mine) + dot_nt(spread_low[...], mine)
+        other = lax.rem(group + i, groups)
+        columns = pl.ds(pl.multiple_of(other * 512, 512), 512)
+        sums = dot(spread_high[...], hot_turned[:, columns])
+        for h in range(4):
+            force_near[h] = sums[:, h * 128 : (h + 1) * 128]
+        for turn in range(1, 5):
+            h = lax.rem(me + turn, 4)
+            target = 4 * other + h
+
+            @pl.when(target != me)
+            def _():
+                force_out[target] = force_near[h].astype(BF16)
+                push_to(force_out.at[target], force_in.at[me], force_sems, region, target).start()
+
+    total = force_near[lax.rem(me, 4)] + dot(spread_low[...], hot_turned[:, own_rows])
+    pushed(force_in, force_sems).wait_recv()
     for step in range(1, members):
-        source = lax.rem(me - step + members, members)
-        push_force(force_out, force_in, force_sems, region, me, member_at(step), step).wait_recv()
-        total = total + force_in[source].astype(F32)
+        total = total + force_in[lax.rem(me + step, members)].astype(F32)
     for lo in range(8):
         for c in range(3):
             at = (lo * 3 + c) * 8
             out[c, :, lo * 128 : (lo + 1) * 128] = total[at : at + 8]
 
-    for copy in motion_push + dens_push + column_push + coeff_push:
-        copy.wait_send()
-    for step in range(1, members):
-        push_force(force_out, force_in, force_sems, region, me, member_at(step), step).wait_send()
-
-
-def push_force(force_out, force_in, sems, region, me, target, step):
+    pushed(motion, motion_sems).wait_send()
+    pushed(dens, dens_sems).wait_send()
+    coeff_pushed.wait_send()
+    pushed(force_out, force_sems).wait_send()
+
+
+def push_to(source, target, sems, region, member):
     return pltpu.make_async_remote_copy(
-        src_ref=force_out.at[target],
-        dst_ref=force_in.at[me],
-        send_sem=sems.at[0, step],
-        recv_sem=sems.at[1, step],
-        device_id=(region, target),
+        src_ref=source,
+        dst_ref=target,
+        send_sem=sems.at[0],
+        recv_sem=sems.at[1],
+        device_id=(region, member),
         device_id_type=MESH,
     )
 
@@ -378,15 +390,17 @@
             pltpu.VMEM(near_blocks.shape, BF16),
             pltpu.VMEM((clusters, 16, 16, 32), F32),
             pltpu.VMEM((lanes, 4 * panels), BF16),
+            pltpu.VMEM((4 * panels, lanes), BF16),
+            pltpu.VMEM((panels, 8), F32),
             pltpu.VMEM((members, rows, 128), BF16),
             pltpu.VMEM((rows, lanes), BF16),
             pltpu.VMEM((rows, 128), BF16),
             pltpu.VMEM((3, 8, panels), F32),
             pltpu.VMEM((members, 16, panels // 2), BF16),
             pltpu.VMEM((members * clusters + 1, 8, 128), F32),
-            pltpu.VMEM((members, regions, clusters, 128), BF16),
+            pltpu.VMEM((members * regions, clusters, 128), BF16),
             pltpu.VMEM((members * regions * clusters, 128), F32),
-            pltpu.VMEM((32, 128), F32),
+            pltpu.VMEM((clusters * 32, 128), F32),
             pltpu.VMEM((clusters, 256, 64), BF16),
             pltpu.VMEM((clusters * 16, 128), F32),
             pltpu.VMEM((128, panels), BF16),
@@ -395,14 +409,15 @@
             pltpu.VMEM((8, panels), F32),
             pltpu.VMEM((rows, 4 * panels), BF16),
             pltpu.VMEM((rows, 4 * panels), BF16),
+            pltpu.VMEM((4, rows, 128), F32),
             pltpu.VMEM((members, rows, 128), BF16),
             pltpu.VMEM((members, rows, 128), BF16),
             dma((2,)),
-            dma((2, members)),
-            dma((2, members)),
-            dma((2, members)),
-            dma((2, regions)),
-            dma((2, members)),
+            dma((2,)),
+            dma((2,)),
+            dma((2,)),
+            dma((2,)),
+            pltpu.SemaphoreType.REGULAR,
         ],
         compiler_params=pltpu.CompilerParams(
             collective_id=0, has_side_effects=True, vmem_limit_bytes=56 * 1024 * 1024

time: 61.3 us -> 57.4 us (0.936)
  Pallas kernels: 58.9 us -> 54.9 us
    pallas_call x1, Pallas kernels: 58.9 us -> 54.9 us  [body(): pl.pallas_call(functools.partial(kernel, regions, members), out_shape=jax...]
where the time goes in v2:
time: 57.4 us; the launch traced here: 56.4 us
  Pallas kernels  54.9 us (96%)
  local copies, waits for them, and re-layouts  1.54 us (3%)
    pallas_call x1, Pallas kernels, body(): pl.pallas_call(functools.partial(kernel, regions, members), out_shape=jax...  54.9 us
    unnamed x1, local copies, waits for them, and re-layouts  1.54 us

profile of v2, /device:TPU:0, one launch (start us, length us, event | category | flops | bytes accessed | tf_op | source)
XLA Modules:
  0.0 56.4 jit_solution(9919190838584067483)
XLA Ops:
  0.0 54.9 %hull.1 = f32[3,8,1024]{2,1,0:T(8,128)} custom-call(s32[16,16]{1,0:T(8,128)} %near_cols.1, s32[16]{0:T(128)} %near_count.1, s32[16,32]{1,0:T(8,128)} %far_cols.1, f32[3,8,1024]{2,1,0:T(8,128)} %bitcast.10, f32[3,1024]{1,0:T(4,128)} %normals.1, f32[1,1024]{1,0:T(1,128)} %bitcast.13, s32[4,1024]{1,0:T(4,128)} %bitcast.12, bf16[16,16,64]{2,1,0:T(8,128)(2,1)} %bitcast.11, ...), custom_call_target="tpu_custom_call" | custom-call | tf_op jit(solution)/shard_map/hull/pallas_call | solution.py:384
  54.9 1.5 %copy.13 = f32[8,3,1024]{2,0,1:T(8,128)} copy(f32[8,3,1024]{2,0,1:T(8,128)} %bitcast.8) | data formatting | bytes 196608

commit v3 on v2

--- a/solution.py
+++ b/solution.py
@@ -61,20 +61,28 @@
     basis_u_high,
     basis_u_low,
     near_pot,
-    spread_high,
-    spread_low,
-    force_near,
+    spread,
     force_out,
-    force_in,
+    upper_own,
+    lower_own,
+    upper_in,
+    lower_in,
+    last_out,
+    last_in,
     load_sems,
     motion_sems,
+    relay_sems,
     dens_sems,
     coeff_sems,
+    side_sems,
     force_sems,
+    last_sems,
     ready,
 ):
     region = lax.axis_index("region")
     me = lax.axis_index("member")
+    x, y = me // 4, lax.rem(me, 4)
+    plane, core = region // 2, lax.rem(region, 2)
     clusters, block = near.shape[0], near.shape[1]
     panels = nodes.shape[1]
     loads = velocity.shape[1]
@@ -111,10 +119,23 @@
         [velocity[c, :, lo * 128 : (lo + 1) * 128] for lo in range(8) for c in range(3)], axis=0
     )
     own_high, own_low = split(own)
-    motion[me] = own_high
+    motion[x, y] = own_high
     motion_low[...] = own_low
     pl.semaphore_wait(barrier, members - 1 + regions - 1)
-    push_all(motion, motion_sems)
+    half_rows = motion.shape[2] // 2
+    upper, lower = pl.ds(0, half_rows), pl.ds(half_rows, half_rows)
+
+    def along_x(turn):
+        return lax.rem(x + turn, 4) * 4 + y
+
+    def along_y(turn):
+        return x * 4 + lax.rem(y + turn, 4)
+
+    for turn in (2, 1, 3):
+        mine = motion.at[x, y, upper]
+        push_to(mine, mine, motion_sems, region, along_x(turn)).start()
+        mine = motion.at[x, y, lower]
+        push_to(mine, mine, motion_sems, region, along_y(turn)).start()
     for step in range(1, regions):
         pl.semaphore_signal(
             ready, inc=1, device_id=(lax.rem(region + step, regions), me), device_id_type=MESH
@@ -122,7 +143,10 @@
 
     node = nodes[...]
     lanes_low, owner = (node & 127).astype(F32), (node >> 10).astype(F32)
-    column_of[...] = jnp.transpose(jnp.concatenate([lanes_low, owner], axis=0))
+    ahead_x = ((node >> 12) - x) & 3
+    ahead_y = (((node >> 10) & 3) - y) & 3
+    stand = (((ahead_y - ahead_x + 3) & 3) * 4 + ahead_x).astype(F32)
+    column_of[...] = jnp.transpose(jnp.concatenate([lanes_low, stand], axis=0))
     one, zero = jnp.ones((), BF16), jnp.zeros((), BF16)
 
     @pl.loop(0, 8)
@@ -137,6 +161,17 @@
                 hot[pl.ds(m * 128 + base, 16), k * panels : (k + 1) * panels] = jnp.where(
                     holder == float(m), found, zero
                 )
+
+    firsts = motion.at[0, pl.ds(0, 3)]
+    first_pushed = push(firsts, firsts, motion_sems, 1)
+    first_pushed.wait_recv()
+    for turn in (2, 1, 3):
+        line = motion.at[:, y, upper]
+        push_to(line, line, relay_sems, region, along_y(turn)).start()
+        line = motion.at[x, :, lower]
+        push_to(line, line, relay_sems, region, along_x(turn)).start()
+    seconds = motion.at[pl.ds(0, 3)]
+    second_pushed = push(seconds, seconds, relay_sems, 1)
 
     @pl.loop(0, panels // 16)
     def _(i):
@@ -172,9 +207,9 @@
 
     table[table.shape[0] - 1] = jnp.zeros((8, 128), F32)
 
-    pushed(motion, motion_sems).wait_recv()
+    second_pushed.wait_recv()
     for m in range(members):
-        motion_cat[:, m * 128 : (m + 1) * 128] = motion[m]
+        motion_cat[:, m * 128 : (m + 1) * 128] = motion[m // 4, m % 4]
     own_rows = pl.ds(pl.multiple_of(me * 128, 128), 128)
 
     for c in range(3):
@@ -208,13 +243,14 @@
     row_load = lax.broadcasted_iota(jnp.int32, (128, 128), 0) & 7
     lane_load = lax.broadcasted_iota(jnp.int32, (128, 128), 1) >> 4
     wide = jnp.where(row_load == lane_load, wide, 0.0)
-    device = region * members + me
+    device = (core * (regions // 2) + plane) * members + me
     coeffs[device] = jnp.sum(wide.reshape(clusters, 8, 128), axis=1).astype(BF16)
     pl.semaphore_wait(ready, regions - 1)
-
-    @pl.loop(1, regions * members)
+    chips = regions // 2 * members
+
+    @pl.loop(1, chips)
     def _(step):
-        there = lax.rem(region + step // members, regions)
+        there = lax.rem(plane + step // members, regions // 2) * 2 + core
         push_to(coeffs.at[device], coeffs.at[device], coeff_sems, there, member_at(lax.rem(step, members))).start()
 
     near_load.wait()
@@ -235,8 +271,7 @@
     slots = near_cols.shape[1]
     unused = table.shape[0] - 1
 
-    @pl.loop(0, clusters // 2)
-    def _(g):
+    def near_pair(g):
         picked = []
         for h in range(2):
             t = 2 * g + h
@@ -252,15 +287,23 @@
         result = dot_nt(both, blocks)
         near_pot[:, pl.ds(pl.multiple_of(g * 128, 128), 128)] = jnp.where(left, result[:8], result[8:])
 
-    coeff_part = coeffs.at[pl.ds(0, regions * members - 1)]
+    pl.loop(0, clusters // 4)(near_pair)
+
+    coeff_part = coeffs.at[pl.ds(0, chips - 1)]
     coeff_pushed = push(coeff_part, coeff_part, coeff_sems, 1)
     coeff_pushed.wait_recv()
+    side = coeffs.at[pl.ds(pl.multiple_of(core * chips, chips), chips)]
+    side_pushed = push_to(side, side, side_sems, region + 1 - 2 * core, me)
+    side_pushed.start()
+    pl.loop(clusters // 4, clusters // 2)(near_pair)
+
+    side_pushed.wait_recv()
 
     @pl.loop(0, members)
     def _(i):
         for r in range(regions):
-            d = i * regions + r
-            at = pl.multiple_of(d * clusters, clusters)
+            at = pl.multiple_of((r * members + i) * clusters, clusters)
+            d = (r % 2 * (regions // 2) + r // 2) * members + i
             coeff_rows[pl.ds(at, clusters), :] = coeffs[d].astype(F32)
 
     own_q = lax.broadcasted_iota(jnp.int32, (256, 128), 0) & 15
@@ -309,41 +352,85 @@
                 rows += [jnp.where(hit, load[c], 0.0) for c in range(3)]
             high, low = split(jnp.concatenate(rows, axis=0))
             columns = pl.ds(k * panels + base, 256)
-            spread_high[:, columns] = high
-            spread_low[:, columns] = low
-
-    groups = members // 4
-    group = me // 4
-
-    @pl.loop(1, groups + 1)
+            spread[0, :, columns] = high
+            spread[1, :, columns] = low
+
+    @pl.loop(0, 5)
     def _(i):
-        other = lax.rem(group + i, groups)
-        columns = pl.ds(pl.multiple_of(other * 512, 512), 512)
-        sums = dot(spread_high[...], hot_turned[:, columns])
-        for h in range(4):
-            force_near[h] = sums[:, h * 128 : (h + 1) * 128]
-        for turn in range(1, 5):
-            h = lax.rem(me + turn, 4)
-            target = 4 * other + h
-
-            @pl.when(target != me)
-            def _():
-                force_out[target] = force_near[h].astype(BF16)
-                push_to(force_out.at[target], force_in.at[me], force_sems, region, target).start()
-
-    total = force_near[lax.rem(me, 4)] + dot(spread_low[...], hot_turned[:, own_rows])
-    pushed(force_in, force_sems).wait_recv()
-    for step in range(1, members):
-        total = total + force_in[lax.rem(me + step, members)].astype(F32)
+        columns = pl.ds(pl.multiple_of((i - i // 4) * 512, 512), 512)
+        sums = dot(spread[i // 4], hot_turned[:, columns])
+
+        @pl.when(i < 4)
+        def _():
+            for h in range(4):
+                ahead = lax.rem(h + i + 1, 4)
+                to_x, to_y = lax.rem(x + h, 4), lax.rem(y + ahead, 4)
+                at = i * 4 + h
+                sums_of = sums[:, h * 128 : (h + 1) * 128]
+                force_out[at] = sums_of.astype(BF16)
+                if h == 0:
+                    upper_own[to_y] = sums_of[:half_rows]
+                else:
+                    push_to(
+                        force_out.at[at, upper], upper_in.at[x, to_y], force_sems, region, to_x * 4 + y
+                    ).start()
+
+                @pl.when(ahead == 0)
+                def _():
+                    lower_own[to_x] = sums_of[half_rows:]
+
+                @pl.when(ahead != 0)
+                def _():
+                    push_to(
+                        force_out.at[at, lower], lower_in.at[y, to_x], force_sems, region, x * 4 + to_y
+                    ).start()
+
+        @pl.when(i == 4)
+        def _():
+            upper_own[y] += sums[:half_rows, :128]
+            lower_own[x] += sums[half_rows:, :128]
+
+    partial = force_out.at[pl.ds(0, 12)]
+    partial_pushed = push(partial, partial, force_sems, 1)
+    partial_pushed.wait_recv()
+
+    def upper_sum(to_y):
+        total = upper_own[to_y]
+        for turn in range(1, 4):
+            total = total + upper_in[lax.rem(x + turn, 4), to_y].astype(F32)
+        return total
+
+    def lower_sum(to_x):
+        total = lower_own[to_x]
+        for turn in range(1, 4):
+            total = total + lower_in[lax.rem(y + turn, 4), to_x].astype(F32)
+        return total
+
+    for turn in (2, 1, 3):
+        last_out[turn, upper] = upper_sum(lax.rem(y + turn, 4)).astype(BF16)
+        piece = (last_out.at[turn, upper], last_in.at[turn, upper])
+        push_to(*piece, last_sems, region, along_y(turn)).start()
+        last_out[turn, lower] = lower_sum(lax.rem(x + turn, 4)).astype(BF16)
+        piece = (last_out.at[turn, lower], last_in.at[turn, lower])
+        push_to(*piece, last_sems, region, along_x(turn)).start()
+    total = jnp.concatenate([upper_sum(y), lower_sum(x)], axis=0)
+    last = last_out.at[pl.ds(1, 3)]
+    last_pushed = push(last, last, last_sems, 1)
+    last_pushed.wait_recv()
+    for turn in range(1, 4):
+        total = total + last_in[turn].astype(F32)
     for lo in range(8):
         for c in range(3):
             at = (lo * 3 + c) * 8
             out[c, :, lo * 128 : (lo + 1) * 128] = total[at : at + 8]
 
-    pushed(motion, motion_sems).wait_send()
+    first_pushed.wait_send()
+    second_pushed.wait_send()
     pushed(dens, dens_sems).wait_send()
     coeff_pushed.wait_send()
-    pushed(force_out, force_sems).wait_send()
+    side_pushed.wait_send()
+    partial_pushed.wait_send()
+    last_pushed.wait_send()
 
 
 def push_to(source, target, sems, region, member):
@@ -392,7 +479,7 @@
             pltpu.VMEM((lanes, 4 * panels), BF16),
             pltpu.VMEM((4 * panels, lanes), BF16),
             pltpu.VMEM((panels, 8), F32),
-            pltpu.VMEM((members, rows, 128), BF16),
+            pltpu.VMEM((4, 4, rows, 128), BF16),
             pltpu.VMEM((rows, lanes), BF16),
             pltpu.VMEM((rows, 128), BF16),
             pltpu.VMEM((3, 8, panels), F32),
@@ -407,11 +494,17 @@
             pltpu.VMEM((clusters * 16, panels), BF16),
             pltpu.VMEM((clusters * 16, panels), BF16),
             pltpu.VMEM((8, panels), F32),
-            pltpu.VMEM((rows, 4 * panels), BF16),
-            pltpu.VMEM((rows, 4 * panels), BF16),
-            pltpu.VMEM((4, rows, 128), F32),
+            pltpu.VMEM((2, rows, 4 * panels), BF16),
             pltpu.VMEM((members, rows, 128), BF16),
-            pltpu.VMEM((members, rows, 128), BF16),
+            pltpu.VMEM((4, rows // 2, 128), F32),
+            pltpu.VMEM((4, rows // 2, 128), F32),
+            pltpu.VMEM((4, 4, rows // 2, 128), BF16),
+            pltpu.VMEM((4, 4, rows // 2, 128), BF16),
+            pltpu.VMEM((4, rows, 128), BF16),
+            pltpu.VMEM((4, rows, 128), BF16),
+            dma((2,)),
+            dma((2,)),
+            dma((2,)),
             dma((2,)),
             dma((2,)),
             dma((2,)),

time: 57.4 us -> 54.3 us (0.946)
  Pallas kernels: 54.9 us -> 52.2 us
    pallas_call x1, Pallas kernels: 54.9 us -> 52.2 us  [body(): pl.pallas_call(functools.partial(kernel, regions, members), out_shape=jax...]
where the time goes in v3:
time: 54.3 us; the launch traced here: 53.7 us
  Pallas kernels  52.2 us (96%)
  local copies, waits for them, and re-layouts  1.54 us (3%)
    pallas_call x1, Pallas kernels, body(): pl.pallas_call(functools.partial(kernel, regions, members), out_shape=jax...  52.2 us
    unnamed x1, local copies, waits for them, and re-layouts  1.54 us

profile of v3, /device:TPU:0, one launch (start us, length us, event | category | flops | bytes accessed | tf_op | source)
XLA Modules:
  0.0 53.7 jit_solution(15518202969564976023)
XLA Ops:
  0.0 52.2 %hull.1 = f32[3,8,1024]{2,1,0:T(8,128)} custom-call(s32[16,16]{1,0:T(8,128)} %near_cols.1, s32[16]{0:T(128)} %near_count.1, s32[16,32]{1,0:T(8,128)} %far_cols.1, f32[3,8,1024]{2,1,0:T(8,128)} %bitcast.10, f32[3,1024]{1,0:T(4,128)} %normals.1, f32[1,1024]{1,0:T(1,128)} %bitcast.13, s32[4,1024]{1,0:T(4,128)} %bitcast.12, bf16[16,16,64]{2,1,0:T(8,128)(2,1)} %bitcast.11, ...), custom_call_target="tpu_custom_call" | custom-call | tf_op jit(solution)/shard_map/hull/pallas_call | solution.py:471
  52.2 1.5 %copy.13 = f32[8,3,1024]{2,0,1:T(8,128)} copy(f32[8,3,1024]{2,0,1:T(8,128)} %bitcast.8) | data formatting | bytes 196608

commit v4 on v3

--- a/solution.py
+++ b/solution.py
@@ -29,6 +29,18 @@
 def kernel(
     regions,
     members,
+    near_cols_hbm,
+    near_count_hbm,
+    far_cols_hbm,
+    velocity_hbm,
+    normals_hbm,
+    areas_hbm,
+    nodes_hbm,
+    basis_v_hbm,
+    basis_u_hbm,
+    near_hbm,
+    coupling_hbm,
+    out,
     near_cols,
     near_count,
     far_cols,
@@ -38,9 +50,6 @@
     nodes,
     basis_v,
     basis_u,
-    near_hbm,
-    coupling_hbm,
-    out,
     near,
     coupling,
     hot,
@@ -90,11 +99,23 @@
     def member_at(step):
         return lax.rem(me + step, members)
 
-    near_load = pltpu.make_async_copy(near_hbm, near, load_sems.at[0])
-    coup_load = pltpu.make_async_copy(coupling_hbm, coupling, load_sems.at[1])
-    near_load.start()
-    coup_load.start()
-
+    def load(source, target, at):
+        return pltpu.make_async_copy(source, target, load_sems.at[at])
+
+    velocity_load = load(velocity_hbm, velocity, 0)
+    nodes_load = load(nodes_hbm, nodes, 1)
+    near_load = load(near_hbm, near, 2)
+    coup_load = load(coupling_hbm, coupling, 3)
+    small_loads = [
+        load(normals_hbm, normals, 4),
+        load(areas_hbm, areas, 5),
+        load(basis_v_hbm, basis_v, 6),
+        load(basis_u_hbm, basis_u, 7),
+        load(near_cols_hbm, near_cols, 8),
+        load(near_count_hbm, near_count, 9),
+        load(far_cols_hbm, far_cols, 10),
+    ]
+    velocity_load.start()
     barrier = pltpu.get_barrier_semaphore()
     for step in range(1, members):
         pl.semaphore_signal(barrier, inc=1, device_id=(region, member_at(step)), device_id_type=MESH)
@@ -103,6 +124,12 @@
             barrier, inc=1, device_id=(lax.rem(region + step, regions), me), device_id_type=MESH
         )
 
+    nodes_load.start()
+    near_load.start()
+    coup_load.start()
+    for copy in small_loads:
+        copy.start()
+
     def push(source, target, sems, step):
         return push_to(source, target, sems, region, member_at(step))
 
@@ -115,6 +142,7 @@
         part = rows.at[pl.ds(0, members - 1)]
         return push(part, part, sems, 1)
 
+    velocity_load.wait()
     own = jnp.concatenate(
         [velocity[c, :, lo * 128 : (lo + 1) * 128] for lo in range(8) for c in range(3)], axis=0
     )
@@ -141,6 +169,7 @@
             ready, inc=1, device_id=(lax.rem(region + step, regions), me), device_id_type=MESH
         )
 
+    nodes_load.wait()
     node = nodes[...]
     lanes_low, owner = (node & 127).astype(F32), (node >> 10).astype(F32)
     ahead_x = ((node >> 12) - x) & 3
@@ -186,6 +215,8 @@
                     holder == float(m), found, zero
                 )
 
+    for copy in small_loads:
+        copy.wait()
     for g in range(clusters // 2):
         pair = jnp.concatenate([basis_v[2 * g], basis_v[2 * g + 1]], axis=1)
         basis_v_wide[:, g * 128 : (g + 1) * 128] = jnp.concatenate([pair] * loads, axis=0)
@@ -233,8 +264,6 @@
     density = normal_vel.astype(BF16).astype(F32)
     half = panels // 2
     dens[me] = jnp.concatenate([density[:, :half], density[:, half:]], axis=0).astype(BF16)
-    push_all(dens, dens_sems)
-
     lane_cluster = lax.broadcasted_iota(jnp.int32, (8, panels), 1) // block
     diagonal = jnp.concatenate(
         [jnp.where(lane_cluster == t, density, 0.0) for t in range(clusters)], axis=0
@@ -253,6 +282,14 @@
         there = lax.rem(plane + step // members, regions // 2) * 2 + core
         push_to(coeffs.at[device], coeffs.at[device], coeff_sems, there, member_at(lax.rem(step, members))).start()
 
+    push_all(dens, dens_sems)
+
+    coeff_part = coeffs.at[pl.ds(0, chips - 1)]
+    coeff_pushed = push(coeff_part, coeff_part, coeff_sems, 1)
+    coeff_pushed.wait_recv()
+    side = coeffs.at[pl.ds(pl.multiple_of(core * chips, chips), chips)]
+    side_pushed = push_to(side, side, side_sems, region + 1 - 2 * core, me)
+    side_pushed.start()
     near_load.wait()
     pushed(dens, dens_sems).wait_recv()
     left = lax.broadcasted_iota(jnp.int32, (8, 128), 1) < block
@@ -287,15 +324,9 @@
         result = dot_nt(both, blocks)
         near_pot[:, pl.ds(pl.multiple_of(g * 128, 128), 128)] = jnp.where(left, result[:8], result[8:])
 
-    pl.loop(0, clusters // 4)(near_pair)
-
-    coeff_part = coeffs.at[pl.ds(0, chips - 1)]
-    coeff_pushed = push(coeff_part, coeff_part, coeff_sems, 1)
-    coeff_pushed.wait_recv()
-    side = coeffs.at[pl.ds(pl.multiple_of(core * chips, chips), chips)]
-    side_pushed = push_to(side, side, side_sems, region + 1 - 2 * core, me)
-    side_pushed.start()
-    pl.loop(clusters // 4, clusters // 2)(near_pair)
+    @pl.loop(0, clusters // 2, unroll=4)
+    def _(g):
+        near_pair(g)
 
     side_pushed.wait_recv()
 
@@ -464,16 +495,24 @@
     clusters, block = near_blocks.shape[0], near_blocks.shape[1]
     rows = 24 * nodes // 128
     lanes = members * 128
-    smem = pl.BlockSpec(memory_space=pltpu.SMEM)
     vmem = pl.BlockSpec(memory_space=pltpu.VMEM)
     hbm = pl.BlockSpec(memory_space=pl.ANY)
     dma = pltpu.SemaphoreType.DMA
     result = pl.pallas_call(
         functools.partial(kernel, regions, members),
-        out_shape=jax.ShapeDtypeStruct((3, 8, nodes), F32),
-        in_specs=[smem] * 3 + [vmem] * 6 + [hbm] * 2,
+        out_shape=pltpu.VMEM((3, 8, nodes), F32),
+        in_specs=[hbm] * 11,
         out_specs=vmem,
         scratch_shapes=[
+            pltpu.SMEM(near_cols.shape, jnp.int32),
+            pltpu.SMEM(near_count.shape, jnp.int32),
+            pltpu.SMEM(far_cols.shape, jnp.int32),
+            pltpu.VMEM((3, 8, nodes), F32),
+            pltpu.VMEM(normals.shape, F32),
+            pltpu.VMEM((1, panels), F32),
+            pltpu.VMEM((4, panels), jnp.int32),
+            pltpu.VMEM((clusters, 16, block), BF16),
+            pltpu.VMEM((clusters, 16, block), F32),
             pltpu.VMEM(near_blocks.shape, BF16),
             pltpu.VMEM((clusters, 16, 16, 32), F32),
             pltpu.VMEM((lanes, 4 * panels), BF16),
@@ -502,7 +541,7 @@
             pltpu.VMEM((4, 4, rows // 2, 128), BF16),
             pltpu.VMEM((4, rows, 128), BF16),
             pltpu.VMEM((4, rows, 128), BF16),
-            dma((2,)),
+            dma((11,)),
             dma((2,)),
             dma((2,)),
             dma((2,)),

time: 54.3 us -> 51.3 us (0.945)
  Pallas kernels: 52.2 us -> 50.5 us
  local copies, waits for them, and re-layouts: 1.54 us -> 0.64 us
    pallas_call x1, Pallas kernels: 52.2 us -> 50.5 us  [body(): pl.pallas_call(functools.partial(kernel, regions, members), out_shape=plt...]
    unnamed x1, local copies, waits for them, and re-layouts: 1.54 us -> 0.64 us
where the time goes in v4:
time: 51.3 us; the launch traced here: 51.2 us
  Pallas kernels  50.5 us (98%)
  local copies, waits for them, and re-layouts  0.64 us (1%)
    pallas_call x1, Pallas kernels, body(): pl.pallas_call(functools.partial(kernel, regions, members), out_shape=plt...  50.5 us

profile of v4, /device:TPU:0, one launch (start us, length us, event | category | flops | bytes accessed | tf_op | source)
XLA Modules:
  0.0 51.2 jit_solution(4892233496743096163)
XLA Ops:
  0.0 50.5 %hull.1 = f32[3,8,1024]{2,1,0:T(8,128)S(1)} custom-call(s32[16,16]{1,0:T(8,128)} %near_cols_hbm.1, s32[16]{0:T(128)} %near_count_hbm.1, s32[16,32]{1,0:T(8,128)} %far_cols_hbm.1, f32[3,8,1024]{2,1,0:T(8,128)} %bitcast.10, f32[3,1024]{1,0:T(4,128)} %normals_hbm.1, f32[1,1024]{1,0:T(1,128)} %bitcast.13, s32[4,1024]{1,0:T(4,128)} %bitcast.12, ...), custom_call_target="tpu_custom_call" | custom-call | tf_op jit(solution)/shard_map/hull/pallas_call | solution.py:501
  50.5 0.6 %copy.13 = f32[8,3,1024]{2,0,1:T(8,128)} copy(f32[8,3,1024]{2,0,1:T(8,128)S(1)} %bitcast.7) | data formatting | bytes 196608

commit v5 on v4

--- a/solution.py
+++ b/solution.py
@@ -99,6 +99,12 @@
     def member_at(step):
         return lax.rem(me + step, members)
 
+    def along_x(turn):
+        return lax.rem(x + turn, 4) * 4 + y
+
+    def along_y(turn):
+        return x * 4 + lax.rem(y + turn, 4)
+
     def load(source, target, at):
         return pltpu.make_async_copy(source, target, load_sems.at[at])
 
@@ -117,8 +123,9 @@
     ]
     velocity_load.start()
     barrier = pltpu.get_barrier_semaphore()
-    for step in range(1, members):
-        pl.semaphore_signal(barrier, inc=1, device_id=(region, member_at(step)), device_id_type=MESH)
+    for turn in range(1, 4):
+        for peer in (along_x(turn), along_y(turn)):
+            pl.semaphore_signal(barrier, inc=1, device_id=(region, peer), device_id_type=MESH)
     for step in range(1, regions):
         pl.semaphore_signal(
             barrier, inc=1, device_id=(lax.rem(region + step, regions), me), device_id_type=MESH
@@ -149,25 +156,15 @@
     own_high, own_low = split(own)
     motion[x, y] = own_high
     motion_low[...] = own_low
-    pl.semaphore_wait(barrier, members - 1 + regions - 1)
+    pl.semaphore_wait(barrier, 6 + regions - 1)
     half_rows = motion.shape[2] // 2
     upper, lower = pl.ds(0, half_rows), pl.ds(half_rows, half_rows)
-
-    def along_x(turn):
-        return lax.rem(x + turn, 4) * 4 + y
-
-    def along_y(turn):
-        return x * 4 + lax.rem(y + turn, 4)
 
     for turn in (2, 1, 3):
         mine = motion.at[x, y, upper]
         push_to(mine, mine, motion_sems, region, along_x(turn)).start()
         mine = motion.at[x, y, lower]
         push_to(mine, mine, motion_sems, region, along_y(turn)).start()
-    for step in range(1, regions):
-        pl.semaphore_signal(
-            ready, inc=1, device_id=(lax.rem(region + step, regions), me), device_id_type=MESH
-        )
 
     nodes_load.wait()
     node = nodes[...]
@@ -199,6 +196,10 @@
         push_to(line, line, relay_sems, region, along_y(turn)).start()
         line = motion.at[x, :, lower]
         push_to(line, line, relay_sems, region, along_x(turn)).start()
+    for step in range(1, regions):
+        pl.semaphore_signal(
+            ready, inc=1, device_id=(lax.rem(region + step, regions), me), device_id_type=MESH
+        )
     seconds = motion.at[pl.ds(0, 3)]
     second_pushed = push(seconds, seconds, relay_sems, 1)
 
@@ -278,7 +279,8 @@
     chips = regions // 2 * members
 
     @pl.loop(1, chips)
-    def _(step):
+    def _(turn):
+        step = chips - turn
         there = lax.rem(plane + step // members, regions // 2) * 2 + core
         push_to(coeffs.at[device], coeffs.at[device], coeff_sems, there, member_at(lax.rem(step, members))).start()
 
@@ -324,7 +326,7 @@
         result = dot_nt(both, blocks)
         near_pot[:, pl.ds(pl.multiple_of(g * 128, 128), 128)] = jnp.where(left, result[:8], result[8:])
 
-    @pl.loop(0, clusters // 2, unroll=4)
+    @pl.loop(0, clusters // 2, unroll=8)
     def _(g):
         near_pair(g)
 
@@ -371,23 +373,56 @@
     for c in range(3):
         moved[c] = potential * (scaled * normals[c : c + 1, :])
 
-    @pl.loop(0, panels // 256)
-    def _(i):
-        base = pl.multiple_of(i * 256, 256)
-        load = [moved[c, :, pl.ds(base, 256)] for c in range(3)]
-        for k in range(4):
-            lo = (nodes[k : k + 1, pl.ds(base, 256)] >> 7) & 7
-            rows = []
-            for q in range(8):
-                hit = jnp.broadcast_to(lo == q, (8, 256))
-                rows += [jnp.where(hit, load[c], 0.0) for c in range(3)]
-            high, low = split(jnp.concatenate(rows, axis=0))
-            columns = pl.ds(k * panels + base, 256)
-            spread[0, :, columns] = high
-            spread[1, :, columns] = low
+    def build_spread(at):
+        @pl.loop(0, panels // 256)
+        def _(i):
+            base = pl.multiple_of(i * 256, 256)
+            load = [moved[c, :, pl.ds(base, 256)] for c in range(3)]
+            for k in range(4):
+                lo = (nodes[k : k + 1, pl.ds(base, 256)] >> 7) & 7
+                rows = []
+                for q in range(8):
+                    hit = jnp.broadcast_to(lo == q, (8, 256))
+                    rows += [jnp.where(hit, load[c], 0.0) for c in range(3)]
+                columns = pl.ds(k * panels + base, 256)
+                spread[at, :, columns] = jnp.concatenate(rows, axis=0).astype(BF16)
+
+    build_spread(0)
+
+    partial = force_out.at[pl.ds(0, 12)]
+    partial_pushed = push(partial, partial, force_sems, 1)
+
+    def upper_sum(to_y):
+        total = upper_own[to_y]
+        for turn in range(1, 4):
+            total = total + upper_in[lax.rem(x + turn, 4), to_y].astype(F32)
+        return total
+
+    def lower_sum(to_x):
+        total = lower_own[to_x]
+        for turn in range(1, 4):
+            total = total + lower_in[lax.rem(y + turn, 4), to_x].astype(F32)
+        return total
+
+    def second_hop():
+        partial_pushed.wait_recv()
+        for turn in (2, 1, 3):
+            last_out[turn, upper] = upper_sum(lax.rem(y + turn, 4)).astype(BF16)
+            piece = (last_out.at[turn, upper], last_in.at[turn, upper])
+            push_to(*piece, last_sems, region, along_y(turn)).start()
+            last_out[turn, lower] = lower_sum(lax.rem(x + turn, 4)).astype(BF16)
+            piece = (last_out.at[turn, lower], last_in.at[turn, lower])
+            push_to(*piece, last_sems, region, along_x(turn)).start()
 
     @pl.loop(0, 5)
     def _(i):
+        @pl.when(i == 4)
+        def _():
+            second_hop()
+            for c in range(3):
+                moved[c] = moved[c] - moved[c].astype(BF16).astype(F32)
+            build_spread(1)
+
         columns = pl.ds(pl.multiple_of((i - i // 4) * 512, 512), 512)
         sums = dot(spread[i // 4], hot_turned[:, columns])
 
@@ -421,29 +456,6 @@
             upper_own[y] += sums[:half_rows, :128]
             lower_own[x] += sums[half_rows:, :128]
 
-    partial = force_out.at[pl.ds(0, 12)]
-    partial_pushed = push(partial, partial, force_sems, 1)
-    partial_pushed.wait_recv()
-
-    def upper_sum(to_y):
-        total = upper_own[to_y]
-        for turn in range(1, 4):
-            total = total + upper_in[lax.rem(x + turn, 4), to_y].astype(F32)
-        return total
-
-    def lower_sum(to_x):
-        total = lower_own[to_x]
-        for turn in range(1, 4):
-            total = total + lower_in[lax.rem(y + turn, 4), to_x].astype(F32)
-        return total
-
-    for turn in (2, 1, 3):
-        last_out[turn, upper] = upper_sum(lax.rem(y + turn, 4)).astype(BF16)
-        piece = (last_out.at[turn, upper], last_in.at[turn, upper])
-        push_to(*piece, last_sems, region, along_y(turn)).start()
-        last_out[turn, lower] = lower_sum(lax.rem(x + turn, 4)).astype(BF16)
-        piece = (last_out.at[turn, lower], last_in.at[turn, lower])
-        push_to(*piece, last_sems, region, along_x(turn)).start()
     total = jnp.concatenate([upper_sum(y), lower_sum(x)], axis=0)
     last = last_out.at[pl.ds(1, 3)]
     last_pushed = push(last, last, last_sems, 1)

time: 51.3 us -> 50.1 us (0.977)
  Pallas kernels: 50.5 us -> 49.4 us
    pallas_call x1, Pallas kernels: 50.5 us -> 49.4 us  [body(): pl.pallas_call(functools.partial(kernel, regions, members), out_shape=plt...]
where the time goes in v5:
time: 50.1 us; the launch traced here: 50 us
  Pallas kernels  49.4 us (99%)
  local copies, waits for them, and re-layouts  0.64 us (1%)
    pallas_call x1, Pallas kernels, body(): pl.pallas_call(functools.partial(kernel, regions, members), out_shape=plt...  49.4 us

profile of v5, /device:TPU:0, one launch (start us, length us, event | category | flops | bytes accessed | tf_op | source)
XLA Modules:
  0.0 50.0 jit_solution(15908024078704163523)
XLA Ops:
  0.0 49.4 %hull.1 = f32[3,8,1024]{2,1,0:T(8,128)S(1)} custom-call(s32[16,16]{1,0:T(8,128)} %near_cols_hbm.1, s32[16]{0:T(128)} %near_count_hbm.1, s32[16,32]{1,0:T(8,128)} %far_cols_hbm.1, f32[3,8,1024]{2,1,0:T(8,128)} %bitcast.10, f32[3,1024]{1,0:T(4,128)} %normals_hbm.1, f32[1,1024]{1,0:T(1,128)} %bitcast.13, s32[4,1024]{1,0:T(4,128)} %bitcast.12, ...), custom_call_target="tpu_custom_call" | custom-call | tf_op jit(solution)/shard_map/hull/pallas_call | solution.py:513
  49.4 0.6 %copy.13 = f32[8,3,1024]{2,0,1:T(8,128)} copy(f32[8,3,1024]{2,0,1:T(8,128)S(1)} %bitcast.7) | data formatting | bytes 196608

commit v6 on v5

--- a/solution.py
+++ b/solution.py
@@ -278,7 +278,7 @@
     pl.semaphore_wait(ready, regions - 1)
     chips = regions // 2 * members
 
-    @pl.loop(1, chips)
+    @pl.loop(1, chips, unroll=7)
     def _(turn):
         step = chips - turn
         there = lax.rem(plane + step // members, regions // 2) * 2 + core
@@ -296,7 +296,7 @@
     pushed(dens, dens_sems).wait_recv()
     left = lax.broadcasted_iota(jnp.int32, (8, 128), 1) < block
 
-    @pl.loop(0, members)
+    @pl.loop(0, members, unroll=16)
     def _(m):
         rows = dens[m].astype(F32)
         for h in range(2):
@@ -332,7 +332,7 @@
 
     side_pushed.wait_recv()
 
-    @pl.loop(0, members)
+    @pl.loop(0, members, unroll=2)
     def _(i):
         for r in range(regions):
             at = pl.multiple_of((r * members + i) * clusters, clusters)
@@ -343,7 +343,7 @@
     lane_q = lax.broadcasted_iota(jnp.int32, (256, 128), 1) & 15
     same_q = own_q == lane_q
 
-    @pl.loop(0, clusters)
+    @pl.loop(0, clusters, unroll=2)
     def _(t):
         for a in range(32):
             picked_rows[pl.ds(t * 32 + a, 1), :] = coeff_rows[pl.ds(far_cols[t, a], 1), :]

time: 50.1 us -> 49 us (0.978)
  Pallas kernels: 49.4 us -> 48.2 us
    pallas_call x1, Pallas kernels: 49.4 us -> 48.2 us  [body(): pl.pallas_call(functools.partial(kernel, regions, members), out_shape=plt...]
where the time goes in v6:
time: 49 us; the launch traced here: 48.9 us
  Pallas kernels  48.2 us (98%)
  local copies, waits for them, and re-layouts  0.64 us (1%)
    pallas_call x1, Pallas kernels, body(): pl.pallas_call(functools.partial(kernel, regions, members), out_shape=plt...  48.2 us

profile of v6, /device:TPU:0, one launch (start us, length us, event | category | flops | bytes accessed | tf_op | source)
XLA Modules:
  0.0 48.9 jit_solution(3886223552785673066)
XLA Ops:
  0.0 48.2 %hull.1 = f32[3,8,1024]{2,1,0:T(8,128)S(1)} custom-call(s32[16,16]{1,0:T(8,128)} %near_cols_hbm.1, s32[16]{0:T(128)} %near_count_hbm.1, s32[16,32]{1,0:T(8,128)} %far_cols_hbm.1, f32[3,8,1024]{2,1,0:T(8,128)} %bitcast.10, f32[3,1024]{1,0:T(4,128)} %normals_hbm.1, f32[1,1024]{1,0:T(1,128)} %bitcast.13, s32[4,1024]{1,0:T(4,128)} %bitcast.12, ...), custom_call_target="tpu_custom_call" | custom-call | tf_op jit(solution)/shard_map/hull/pallas_call | solution.py:513
  48.3 0.6 %copy.13 = f32[8,3,1024]{2,0,1:T(8,128)} copy(f32[8,3,1024]{2,0,1:T(8,128)S(1)} %bitcast.7) | data formatting | bytes 196608

commit v7 on v6

--- a/solution.py
+++ b/solution.py
@@ -247,7 +247,7 @@
     for c in range(3):
         moved[c] = jnp.zeros((8, panels), F32)
 
-    @pl.loop(0, 4)
+    @pl.loop(0, 4, unroll=2)
     def _(k):
         columns = pl.ds(pl.multiple_of(k * panels, panels), panels)
         rows = dot(motion_cat[...], hot[:, columns]) + dot(motion_low[...], hot[own_rows, columns])

time: 49 us -> 48.7 us (level)
  no operation moved by 1% of the time
where the time goes in v7:
time: 48.7 us; the launch traced here: 48.6 us
  Pallas kernels  48 us (99%)
  local copies, waits for them, and re-layouts  0.64 us (1%)
    pallas_call x1, Pallas kernels, body(): pl.pallas_call(functools.partial(kernel, regions, members), out_shape=plt...  48 us

profile of v7, /device:TPU:0, one launch (start us, length us, event | category | flops | bytes accessed | tf_op | source)
XLA Modules:
  0.0 48.6 jit_solution(15879075666499384401)
XLA Ops:
  0.0 48.0 %hull.1 = f32[3,8,1024]{2,1,0:T(8,128)S(1)} custom-call(s32[16,16]{1,0:T(8,128)} %near_cols_hbm.1, s32[16]{0:T(128)} %near_count_hbm.1, s32[16,32]{1,0:T(8,128)} %far_cols_hbm.1, f32[3,8,1024]{2,1,0:T(8,128)} %bitcast.10, f32[3,1024]{1,0:T(4,128)} %normals_hbm.1, f32[1,1024]{1,0:T(1,128)} %bitcast.13, s32[4,1024]{1,0:T(4,128)} %bitcast.12, ...), custom_call_target="tpu_custom_call" | custom-call | tf_op jit(solution)/shard_map/hull/pallas_call | solution.py:513
  48.0 0.6 %copy.13 = f32[8,3,1024]{2,0,1:T(8,128)} copy(f32[8,3,1024]{2,0,1:T(8,128)S(1)} %bitcast.7) | data formatting | bytes 196608

commit v8 on v6

--- a/solution.py
+++ b/solution.py
@@ -141,7 +141,7 @@
         return push_to(source, target, sems, region, member_at(step))
 
     def push_all(rows, sems):
-        @pl.loop(1, members)
+        @pl.loop(1, members, unroll=5)
         def _(step):
             push(rows.at[me], rows.at[me], sems, step).start()
 
@@ -343,7 +343,7 @@
     lane_q = lax.broadcasted_iota(jnp.int32, (256, 128), 1) & 15
     same_q = own_q == lane_q
 
-    @pl.loop(0, clusters, unroll=2)
+    @pl.loop(0, clusters, unroll=4)
     def _(t):
         for a in range(32):
             picked_rows[pl.ds(t * 32 + a, 1), :] = coeff_rows[pl.ds(far_cols[t, a], 1), :]

time: 49 us -> 49 us (level)
  no operation moved by 1% of the time
where the time goes in v8:
time: 49 us; the launch traced here: 48.9 us
  Pallas kernels  48.2 us (98%)
  local copies, waits for them, and re-layouts  0.64 us (1%)
    pallas_call x1, Pallas kernels, body(): pl.pallas_call(functools.partial(kernel, regions, members), out_shape=plt...  48.2 us

profile of v8, /device:TPU:0, one launch (start us, length us, event | category | flops | bytes accessed | tf_op | source)
XLA Modules:
  0.0 48.9 jit_solution(17066969101056785262)
XLA Ops:
  0.0 48.2 %hull.1 = f32[3,8,1024]{2,1,0:T(8,128)S(1)} custom-call(s32[16,16]{1,0:T(8,128)} %near_cols_hbm.1, s32[16]{0:T(128)} %near_count_hbm.1, s32[16,32]{1,0:T(8,128)} %far_cols_hbm.1, f32[3,8,1024]{2,1,0:T(8,128)} %bitcast.10, f32[3,1024]{1,0:T(4,128)} %normals_hbm.1, f32[1,1024]{1,0:T(1,128)} %bitcast.13, s32[4,1024]{1,0:T(4,128)} %bitcast.12, ...), custom_call_target="tpu_custom_call" | custom-call | tf_op jit(solution)/shard_map/hull/pallas_call | solution.py:513
  48.2 0.6 %copy.13 = f32[8,3,1024]{2,0,1:T(8,128)} copy(f32[8,3,1024]{2,0,1:T(8,128)S(1)} %bitcast.7) | data formatting | bytes 196608
